TPU v7x, 32 devices: a whole 2x2x4 slice. The times are simulated.
32 devices in a mesh: space: 8 (over z, y), bin: 4 (over x, core).
Axes of the slice: x: 2, y: 2, z: 4, core: 2. Of those that a mesh axis runs over, the one named last changes fastest.
Arguments:
- spectrum: float32 [768, 320, 256], P('bin', 'space'), may hold values from 0.05 to 2
- sea_mask: int32 [320, 256], P('space'), may hold values 0 or 1
- wind_speed: float32 [320, 256], P('space'), may hold values from 5 to 25
- wind_heading: float32 [320, 256], P('space'), may hold values from -3.140625 to 3.140625
- quad: bfloat16 [768, 768], replicated, may hold values from -0.21875 to 0.21875
Outputs:
- new_spectrum: float32 [768, 320, 256], P('bin', 'space')
All inputs are finite; a program needn't handle non-finite values. No bound on the sum of `sea_mask` on one device may be relied on, other than what follows from the above.
Results may differ from a plain program's by a relative error of at most 0.0003.
The roundings to bfloat16 on the way count: a program that leaves them out, or rounds other values in their place, can miss the bound.
Values sent between devices are 32-bit elements; how exact they have to be, the bound alone decides.
A program may use at most 128 MiB of HBM per device.

v0:
```python
import math

import jax
import jax.numpy as jnp
from jax import lax
from jax.sharding import PartitionSpec as P

FREQS = 32
DIRS = 24
BINS = 768


LOG_RATIO = math.log(1.1)
TWO_PI = 2.0 * math.pi
TIME_STEP = 0.2
NONLINEAR = 1.5
DAMPING = 2.0
GROWTH = 0.15


def extended(block, sides, width):
    for axis, dim in sides:
        count = lax.axis_size(axis)
        forward = [(i, i + 1) for i in range(count - 1)]
        backward = [(target, source) for source, target in forward]
        low = lax.ppermute(
            lax.slice_in_dim(block, block.shape[dim] - width, None, axis=dim), axis, forward
        )
        high = lax.ppermute(lax.slice_in_dim(block, 0, width, axis=dim), axis, backward)
        block = jnp.concatenate([low, block, high], axis=dim)
    return block


def bin_tables(bin_index):
    freq_level = (bin_index // DIRS).astype(jnp.float32)
    direction = (bin_index % DIRS).astype(jnp.float32)
    frequency = 0.04 * jnp.exp(freq_level * LOG_RATIO)
    courant = 0.65 * jnp.exp(-freq_level * LOG_RATIO)
    theta = (direction + 0.5) * (TWO_PI / DIRS)
    cos_theta = jnp.cos(theta)
    sin_theta = jnp.sin(theta)
    return (frequency, courant * cos_theta, courant * sin_theta, cos_theta, sin_theta)


def substep(padded, sea_rows, x_speed, y_speed):
    center = padded[:, 1:-1]
    back_row = padded[:, :-2]
    next_row = padded[:, 2:]
    sided = jnp.pad(center, ((0, 0), (0, 0), (1, 1)))
    left_col = sided[:, :, :-2]
    right_col = sided[:, :, 2:]
    updated = center - jnp.maximum(x_speed, 0.0) * (center - back_row)
    updated = updated - jnp.minimum(x_speed, 0.0) * (next_row - center)
    updated = updated - jnp.maximum(y_speed, 0.0) * (center - left_col)
    updated = updated - jnp.minimum(y_speed, 0.0) * (right_col - center)
    return updated * sea_rows


def reflect(values):
    count = values.shape[1]
    return values.reshape(FREQS, DIRS, count)[:, ::-1].reshape(FREQS * DIRS, count)


def sources(energy, quad, frequency):
    count = energy.shape[1]
    low = energy.astype(jnp.bfloat16)
    coupled = jnp.dot(
        quad, jnp.concatenate([low, reflect(low)], axis=1), preferred_element_type=jnp.float32
    )
    transfer = NONLINEAR * energy * (coupled[:, :count] + reflect(coupled[:, count:]))
    total = jnp.sum(energy, axis=0) / BINS
    top_freq = 0.04 * math.exp((FREQS - 1) * LOG_RATIO)
    steep = frequency / top_freq
    dissipation = -DAMPING * (steep * steep)[:, None] * energy * (total * total)[None, :]
    return transfer + dissipation


def wind_growth(energy, frequency, cos_theta, sin_theta, speed, heading):
    along = cos_theta * jnp.cos(heading) + sin_theta * jnp.sin(heading)
    rate = GROWTH * jnp.maximum(0.77 * speed * frequency * along - 1.0, 0.0)
    return rate * energy


def column3(values):
    return values[:, None, None]


def on_device(spectrum, sea_mask, wind_speed, wind_heading, quad):
    per_dev, row_count, col_count = spectrum.shape
    bin_index = lax.axis_index("bin") * per_dev + jnp.arange(per_dev, dtype=jnp.int32)
    frequency, x_table, y_table, cos_theta, sin_theta = bin_tables(bin_index)
    x_speed = column3(x_table)
    y_speed = column3(y_table)
    sea_rows = sea_mask.astype(jnp.float32)
    current = spectrum
    for sweep in range(3):
        padded = extended(current, (("space", 1),), 1)
        current = substep(padded, sea_rows, x_speed, y_speed)
    growth = wind_growth(
        current,
        column3(frequency),
        column3(cos_theta),
        column3(sin_theta),
        wind_speed[None],
        wind_heading[None],
    )
    all_frequency = bin_tables(jnp.arange(BINS, dtype=jnp.int32))[0]
    groups = lax.axis_size("bin")
    owned = row_count * col_count // groups
    outgoing = current.reshape(per_dev, groups, owned)
    received = lax.all_to_all(outgoing, "bin", split_axis=1, concat_axis=0, tiled=True)
    returned = lax.all_to_all(
        sources(received[:, 0, :], quad, all_frequency)[:, None, :],
        "bin",
        split_axis=0,
        concat_axis=1,
        tiled=True,
    )
    source = returned.reshape(per_dev, row_count, col_count)
    return current + TIME_STEP * (growth + source)


def solution(mesh):
    return jax.shard_map(
        on_device,
        mesh=mesh,
        in_specs=(
            P("bin", "space", None),
            P("space", None),
            P("space", None),
            P("space", None),
            P(),
        ),
        out_specs=P("bin", "space", None),
        check_vma=False,
    )
```

profile of v0, /device:TPU:1, one launch (start us, length us, event | category | flops | bytes accessed | tf_op | source)
XLA Modules:
  0.0 425.8 jit_solution(3842399228876756901)
XLA Ops:
  0.0 2.3 fusion.68
  2.3 4.0 collective-permute-start
  6.3 1.3 collective-permute-start.1
  8.5 1.3 collective-permute-done
  10.0 3.6 collective-permute-done.1
  13.9 19.5 %fusion.4 = f32[192,40,256]{2,1,0:T(8,128)S(1)} fusion(f32[192,40,256]{2,1,0:T(8,128)} %param.5, f32[192,1,256]{2,1,0:T(1,128)S(1)} %copy.54, f32[192,1,256]{2,1,0:T(1,128)S(1)} %copy.52, f32[40,256]{1,0:T(8,128)S(1)} %convert_element_type.66, f32[192]{0:T(256)S(1)} %get-tuple-element.18, f32[192]{0:T(256)S(1)} %get-tuple-element.19, ...), kind=kLoop, calls=%fused_computation.11 | loop fusion | flops 29491200 | bytes 16165888 | tf_op jit(solution)/shard_map/mul | solution.py:56
  33.7 4.1 collective-permute-start.2
  37.9 1.3 collective-permute-start.3
  39.2 1.3 collective-permute-done.2
  40.6 7.2 %collective-permute-done.3 = f32[192,1,256]{2,0,1:T(8,128)S(1)} collective-permute-done((f32[192,1,256]{2,0,1:T(8,128)S(1)}, f32[192,1,256]{2,0,1:T(8,128)S(1)}, u32[]{:S(2)}, u32[]{:S(2)}) %collective-permute-start.3) | collective-permute-done | bytes 196640 | tf_op jit(solution)/shard_map/ppermute | solution.py:29
  48.0 9.0 %fusion.11 = f32[192,40,256]{2,1,0:T(8,128)S(1)} fusion(f32[192,40,256]{2,1,0:T(8,128)S(1)} %fusion.4, f32[192,1,256]{2,1,0:T(1,128)S(1)} %copy.58, f32[192,1,256]{2,1,0:T(1,128)S(1)} %copy.56, f32[40,256]{1,0:T(8,128)S(1)} %convert_element_type.66, f32[192]{0:T(256)S(1)} %get-tuple-element.18, f32[192]{0:T(256)S(1)} %get-tuple-element.19, ...), kind=kLoop, calls=%fused_computation.18 | loop fusion | flops 29491200 | bytes 16165888 | tf_op jit(solution)/shard_map/mul | solution.py:56
  57.3 3.9 collective-permute-start.4
  61.3 1.3 collective-permute-start.5
  64.1 7.1 %collective-permute-done.5 = f32[192,1,256]{2,0,1:T(8,128)S(1)} collective-permute-done((f32[192,1,256]{2,0,1:T(8,128)S(1)}, f32[192,1,256]{2,0,1:T(8,128)S(1)}, u32[]{:S(2)}, u32[]{:S(2)}) %collective-permute-start.5) | collective-permute-done | bytes 196640 | tf_op jit(solution)/shard_map/ppermute | solution.py:29
  71.4 10.2 %fusion.18 = f32[192,40,256]{2,1,0:T(8,128)} fusion(f32[192,40,256]{2,1,0:T(8,128)S(1)} %fusion.11, f32[192,1,256]{2,1,0:T(1,128)S(1)} %copy.62, f32[192,1,256]{2,1,0:T(1,128)S(1)} %copy.60, f32[40,256]{1,0:T(8,128)S(1)} %convert_element_type.66, f32[192]{0:T(256)S(1)} %get-tuple-element.18, f32[192]{0:T(256)S(1)} %get-tuple-element.19, ...), kind=kLoop, calls=%fused_computation.25 | loop fusion | flops 29491200 | bytes 16165888 | tf_op jit(solution)/shard_map/mul | solution.py:56
  81.5 10.3 %reshape.102 = f32[192,4,2560]{2,1,0:T(4,128)} reshape(f32[192,40,256]{2,1,0:T(8,128)} %fusion.18) | data formatting | bytes 15728640 | tf_op jit(solution)/shard_map/reshape | solution.py:110
  91.9 9.0 %copy.63 = f32[192,4,2560]{2,0,1:T(8,128)} copy(f32[192,4,2560]{2,1,0:T(4,128)} %reshape.102) | data formatting | bytes 15728640 | tf_op jit(solution)/shard_map/reshape | solution.py:110
  100.9 6.9 %all-to-all-start = ((f32[192,4,2560]{2,0,1:T(8,128)}), f32[192,4,2560]{2,0,1:T(8,128)}, u32[]{:S(2)}, u32[]{:S(2)}) async-start(f32[192,4,2560]{2,0,1:T(8,128)} %copy.63), calls=%async_computation | async-start | bytes 15728640 | tf_op jit(solution)/shard_map/all_to_all | solution.py:111
  107.8 86.7 %all-to-all-done = f32[192,4,2560]{2,0,1:T(8,128)} async-done(((f32[192,4,2560]{2,0,1:T(8,128)}), f32[192,4,2560]{2,0,1:T(8,128)}, u32[]{:S(2)}, u32[]{:S(2)}) %all-to-all-start) | async-done | bytes 7864352 | tf_op jit(solution)/shard_map/all_to_all | solution.py:111
  194.5 7.2 %fusion.65 = (f32[2560]{0:T(1024)S(1)}, bf16[768,2560]{1,0:T(8,128)(2,1)}, bf16[4,192,1,2560]{3,1,0,2:T(8,128)(2,1)}) fusion(f32[192,4,2560]{2,0,1:T(8,128)} %all-to-all-done), kind=kLoop, calls=%fused_computation.100 | loop fusion | flops 5895680 | bytes 15738880 | tf_op jit(solution)/shard_map/reduce_sum | solution.py:71
  201.7 12.6 %rev.6 = bf16[32,24,2560]{2,1,0:T(8,128)(2,1)} reverse(bf16[32,24,2560]{2,1,0:T(8,128)(2,1)} %bitcast.33), dimensions={1} | reverse | bytes 7864320 | tf_op jit(solution)/shard_map/rev | solution.py:61
  214.3 8.7 %convolution_bitcast_fusion = f32[768,5120]{1,0:T(8,128)S(1)} fusion(bf16[768,768]{1,0:T(8,128)(2,1)S(1)} %copy-done, bf16[768,2560]{1,0:T(8,128)(2,1)} %bitcast.34, bf16[768,2560]{1,0:T(8,128)(2,1)} %get-tuple-element.6), kind=kOutput, calls=%fused_computation.6 | convolution fusion | flops 6055526400 | bytes 24772608 | tf_op jit(solution)/shard_map/dot_general | solution.py:67
  223.1 4.1 slice.91
  227.2 3.8 copy-done.3
  230.9 13.5 %rev.7 = f32[32,24,2560]{2,1,0:T(8,128)} reverse(f32[32,24,2560]{2,1,0:T(8,128)} %bitcast.32), dimensions={1} | reverse | bytes 15728640 | tf_op jit(solution)/shard_map/rev | solution.py:61
  244.5 9.4 %fusion.23 = f32[768,1,2560]{2,0,1:T(8,128)S(1)} fusion(f32[768,5120]{1,0:T(8,128)} %copy-done.3, f32[32,24,2560]{2,1,0:T(8,128)} %rev.7, f32[192,4,2560]{2,0,1:T(8,128)} %all-to-all-done, f32[2560]{0:T(1024)S(1)} %multiply_multiply_fusion, f32[768]{0:T(1024)S(1)} %fusion.51), kind=kLoop, calls=%fused_computation.31 | loop fusion | flops 11796480 | bytes 31470592 | tf_op jit(solution)/shard_map/broadcast_in_dim | solution.py:113
  253.8 30.1 %copy.64 = f32[768,1,2560]{2,1,0:T(1,128)} copy(f32[768,1,2560]{2,0,1:T(8,128)S(1)} %fusion.23) | data formatting | bytes 15728640 | tf_op jit(solution)/shard_map/broadcast_in_dim | solution.py:113
  283.9 6.5 %all-to-all-start.1 = ((f32[768,1,2560]{2,1,0:T(1,128)}), f32[768,1,2560]{2,1,0:T(1,128)}, u32[]{:S(2)}, u32[]{:S(2)}) async-start(f32[768,1,2560]{2,1,0:T(1,128)} %copy.64), calls=%async_computation.1 | async-start | bytes 15728640 | tf_op jit(solution)/shard_map/all_to_all | solution.py:112
  290.7 86.4 %all-to-all-done.1 = f32[768,1,2560]{2,1,0:T(1,128)} async-done(((f32[768,1,2560]{2,1,0:T(1,128)}), f32[768,1,2560]{2,1,0:T(1,128)}, u32[]{:S(2)}, u32[]{:S(2)}) %all-to-all-start.1) | async-done | bytes 7864352 | tf_op jit(solution)/shard_map/all_to_all | solution.py:112
  377.1 11.5 %copy.69 = f32[4,192,1,2560]{3,0,1,2:T(4,128)} copy(f32[4,192,1,2560]{3,2,1,0:T(1,128)} %bitcast.11) | data formatting | bytes 15728640 | tf_op jit(solution)/shard_map/all_to_all | solution.py:112
  388.6 10.4 %reshape.106 = f32[192,40,256]{2,1,0:T(8,128)} reshape(f32[192,4,1,2560]{3,1,0,2:T(4,128)} %bitcast.31) | data formatting | bytes 15728640 | tf_op jit(solution)/shard_map/reshape | solution.py:119
  399.1 26.8 %multiply_add_fusion = f32[192,40,256]{2,1,0:T(8,128)} fusion(f32[192,40,256]{2,1,0:T(8,128)} %reshape.106, f32[40,256]{1,0:T(8,128)S(1)} %get-tuple-element.15, f32[192]{0:T(256)S(1)} %get-tuple-element.17, f32[40,256]{1,0:T(8,128)S(1)} %get-tuple-element.14, f32[192]{0:T(256)S(1)} %fusion.61, f32[192]{0:T(256)S(1)} %get-tuple-element.16, ...), kind=kLoop, calls=%fused_computation.65 | loop fusion | flops 53084160 | bytes 24155392 | tf_op jit(solution)/shard_map/add | solution.py:120
  (34 shorter events, 4.3 us)
Async XLA Ops:
  0.0 214.3 %copy-start = (bf16[768,768]{1,0:T(8,128)(2,1)S(1)}, bf16[768,768]{1,0:T(8,128)(2,1)}, u32[]{:S(2)}) copy-start(bf16[768,768]{1,0:T(8,128)(2,1)} %param.9) | copy-start | bytes 3538948
  2.3 7.5 %collective-permute-start = (f32[192,1,256]{2,0,1:T(8,128)S(1)}, f32[192,1,256]{2,0,1:T(8,128)S(1)}, u32[]{:S(2)}, u32[]{:S(2)}) collective-permute-start(f32[192,1,256]{2,0,1:T(8,128)S(1)} %copy.66), channel_id=1, source_target_pairs={{0,4},{4,8},{8,12},{12,16},{16,20},{20,24},{24,28},{1,5},{5,9},{9,... | collective-permute-start | bytes 589832 | tf_op jit(solution)/shard_map/ppermute | solution.py:26
  6.3 7.3 %collective-permute-start.1 = (f32[192,1,256]{2,0,1:T(8,128)S(1)}, f32[192,1,256]{2,0,1:T(8,128)S(1)}, u32[]{:S(2)}, u32[]{:S(2)}) collective-permute-start(f32[192,1,256]{2,0,1:T(8,128)S(1)} %copy.67), channel_id=1, source_target_pairs={{4,0},{8,4},{12,8},{16,12},{20,16},{24,20},{28,24},{5,1},{9,5},{13... | collective-permute-start | bytes 589832 | tf_op jit(solution)/shard_map/ppermute | solution.py:29
  33.7 6.7 %collective-permute-start.2 = (f32[192,1,256]{2,0,1:T(8,128)S(1)}, f32[192,1,256]{2,0,1:T(8,128)S(1)}, u32[]{:S(2)}, u32[]{:S(2)}) collective-permute-start(f32[192,1,256]{2,0,1:T(8,128)S(1)} %copy.55), channel_id=1, source_target_pairs={{0,4},{4,8},{8,12},{12,16},{16,20},{20,24},{24,28},{1,5},{5,9},{9,... | collective-permute-start | bytes 589832 | tf_op jit(solution)/shard_map/ppermute | solution.py:26
  37.9 10.0 %collective-permute-start.3 = (f32[192,1,256]{2,0,1:T(8,128)S(1)}, f32[192,1,256]{2,0,1:T(8,128)S(1)}, u32[]{:S(2)}, u32[]{:S(2)}) collective-permute-start(f32[192,1,256]{2,0,1:T(8,128)S(1)} %copy.57), channel_id=1, source_target_pairs={{4,0},{8,4},{12,8},{16,12},{20,16},{24,20},{28,24},{5,1},{9,5},{13... | collective-permute-start | bytes 589832 | tf_op jit(solution)/shard_map/ppermute | solution.py:29
  57.0 14.4 %copy-start.2 = (f32[192,40,256]{2,1,0:T(8,128)}, f32[192,40,256]{2,1,0:T(8,128)S(1)}, u32[]{:S(2)}) copy-start(f32[192,40,256]{2,1,0:T(8,128)S(1)} %fusion.11) | copy-start | bytes 23592964
  57.3 6.5 %collective-permute-start.4 = (f32[192,1,256]{2,0,1:T(8,128)S(1)}, f32[192,1,256]{2,0,1:T(8,128)S(1)}, u32[]{:S(2)}, u32[]{:S(2)}) collective-permute-start(f32[192,1,256]{2,0,1:T(8,128)S(1)} %copy.59), channel_id=1, source_target_pairs={{0,4},{4,8},{8,12},{12,16},{16,20},{20,24},{24,28},{1,5},{5,9},{9,... | collective-permute-start | bytes 589832 | tf_op jit(solution)/shard_map/ppermute | solution.py:26
  61.3 9.9 %collective-permute-start.5 = (f32[192,1,256]{2,0,1:T(8,128)S(1)}, f32[192,1,256]{2,0,1:T(8,128)S(1)}, u32[]{:S(2)}, u32[]{:S(2)}) collective-permute-start(f32[192,1,256]{2,0,1:T(8,128)S(1)} %copy.61), channel_id=1, source_target_pairs={{4,0},{8,4},{12,8},{16,12},{20,16},{24,20},{28,24},{5,1},{9,5},{13... | collective-permute-start | bytes 589832 | tf_op jit(solution)/shard_map/ppermute | solution.py:29
  100.9 93.6 %all-to-all-start = ((f32[192,4,2560]{2,0,1:T(8,128)}), f32[192,4,2560]{2,0,1:T(8,128)}, u32[]{:S(2)}, u32[]{:S(2)}) async-start(f32[192,4,2560]{2,0,1:T(8,128)} %copy.63), calls=%async_computation | async-start | bytes 15728640 | tf_op jit(solution)/shard_map/all_to_all | solution.py:111
  223.1 7.8 %copy-start.3 = (f32[768,5120]{1,0:T(8,128)}, f32[768,5120]{1,0:T(8,128)S(1)}, u32[]{:S(2)}) copy-start(f32[768,5120]{1,0:T(8,128)S(1)} %convolution_bitcast_fusion) | copy-start | bytes 47185924
  283.9 6.6 %copy-start.4 = (f32[40,256]{1,0:T(8,128)S(1)}, f32[40,256]{1,0:T(8,128)}, u32[]{:S(2)}) copy-start(f32[40,256]{1,0:T(8,128)} %param.8) | copy-start | bytes 122884
  283.9 6.6 %copy-start.5 = (f32[40,256]{1,0:T(8,128)S(1)}, f32[40,256]{1,0:T(8,128)}, u32[]{:S(2)}) copy-start(f32[40,256]{1,0:T(8,128)} %param.7) | copy-start | bytes 122884
  283.9 93.2 %all-to-all-start.1 = ((f32[768,1,2560]{2,1,0:T(1,128)}), f32[768,1,2560]{2,1,0:T(1,128)}, u32[]{:S(2)}, u32[]{:S(2)}) async-start(f32[768,1,2560]{2,1,0:T(1,128)} %copy.64), calls=%async_computation.1 | async-start | bytes 15728640 | tf_op jit(solution)/shard_map/all_to_all | solution.py:112
  399.0 26.8 %copy-start.1 = (bf16[768,768]{1,0:T(8,128)(2,1)S(1)}, bf16[768,768]{1,0:T(8,128)(2,1)}, u32[]{:S(2)}) copy-start(bf16[768,768]{1,0:T(8,128)(2,1)} %param.9) | copy-start | bytes 3538948
where the time goes:
time: 429 us; the launch traced here: 426 us
  waiting for transfers between devices  195 us (45%)
  local copies, waits for them, and re-layouts  109 us (25%)
  other arithmetic  83.2 us (19%)
  starting transfers between devices  29.3 us (7%)
  matrix products  8.72 us (2%)
    all_to_all x1, waiting for transfers between devices, on_device(): lax.all_to_all(outgoing, 'bin', split_axis=1, concat_axis=0, tiled=True)  86.7 us
    all_to_all x1, waiting for transfers between devices, on_device(): lax.all_to_all(sources(received[:, 0, :], quad, all_frequency)[:, None, :...  86.4 us
    mul x3, other arithmetic, substep(): return updated * sea_rows  38.7 us
    broadcast_in_dim x1, local copies, waits for them, and re-layouts, on_device(): sources(received[:, 0, :], quad, all_frequency)[:, None, :]  30.1 us
    add x1, other arithmetic, on_device(): return current + TIME_STEP * (growth + source)  26.8 us
    rev x2, local copies, waits for them, and re-layouts, reflect(): values.reshape(FREQS, DIRS, count)[:, ::-1].reshape(FREQS * DIRS, count)  26.1 us
    reshape x2, local copies, waits for them, and re-layouts, on_device(): outgoing = current.reshape(per_dev, groups, owned)  19.3 us
    ppermute x3, waiting for transfers between devices, extended(): lax.ppermute(lax.slice_in_dim(block, 0, width, axis=dim), axis, backward)  17.9 us
  transfers between devices with their start and end apart: 8, of which 8 were waited for; matrix products, arithmetic and copies ran while one was open for 0% of the time, Pallas kernels for 0%

commit v1 on v0

v1 whole, which is shorter than its diff:
```python
import functools
import math

import jax
import jax.numpy as jnp
import numpy as np
from jax import lax
from jax.experimental import pallas as pl
from jax.experimental.pallas import tpu as pltpu
from jax.sharding import PartitionSpec as P

FREQS = 32
DIRS = 24
BINS = 768

LOG_RATIO = math.log(1.1)
TWO_PI = 2.0 * math.pi
TIME_STEP = 0.2
NONLINEAR = 1.5
DAMPING = 2.0
GROWTH = 0.15

HALO = 3
TILE = 8
UNIT = 2

AX, AY, XPOS, YPOS, FCOS, FSIN, STEEP2 = range(7)


def bin_tables():
    bins = np.arange(BINS)
    level = (bins // DIRS).astype(np.float64)
    direction = (bins % DIRS).astype(np.float64)
    frequency = 0.04 * np.exp(level * LOG_RATIO)
    courant = 0.65 * np.exp(-level * LOG_RATIO)
    theta = (direction + 0.5) * (TWO_PI / DIRS)
    cos_theta, sin_theta = np.cos(theta), np.sin(theta)
    top_freq = 0.04 * math.exp((FREQS - 1) * LOG_RATIO)
    table = np.zeros((BINS, 128), np.float32)
    table[:, AX] = np.abs(courant * cos_theta)
    table[:, AY] = np.abs(courant * sin_theta)
    table[:, XPOS] = cos_theta > 0
    table[:, YPOS] = sin_theta > 0
    table[:, FCOS] = frequency * cos_theta
    table[:, FSIN] = frequency * sin_theta
    table[:, STEEP2] = (frequency / top_freq) ** 2
    return table


def reversal(rows, row_start, cols, col_start):
    i = lax.broadcasted_iota(jnp.int32, (rows, cols), 0).astype(jnp.float32) + row_start
    j = lax.broadcasted_iota(jnp.int32, (rows, cols), 1).astype(jnp.float32) + col_start
    level = jnp.floor((i + 0.5) * (1.0 / DIRS))
    return jnp.where(i + j == 2 * DIRS * level + (DIRS - 1), 1.0, 0.0).astype(jnp.bfloat16)


def kernel(
    n, s, spec, mask, speed, heading, quad, table, out,
    ext, mask_s, u_s, v_s, every, q2, tab,
    load_sem, halo_send, halo_recv, x_send, x_recv, f_send, f_recv, out_sem,
):
    rows, nb, cols = spec.shape
    tiles = rows // TILE
    units = rows // UNIT
    chips = n // 2
    b = lax.axis_index("bin")
    sp = lax.axis_index("space")
    chip, core = b // 2, lax.rem(b, 2)
    sibling = chip * 2 + 1 - core

    def far_to(k):
        return lax.rem(chip + k, chips) * 2 + core

    def far_from(k):
        return lax.rem(chip + chips - k, chips) * 2 + core

    loads = [
        pltpu.make_async_copy(
            spec.at[pl.ds(t * TILE, TILE)], ext.at[pl.ds(HALO + t * TILE, TILE)], load_sem.at[t]
        )
        for t in range(tiles)
    ]
    for load in loads:
        load.start()
    tab_load = pltpu.make_async_copy(
        table.at[pl.ds(pl.multiple_of(b * nb, 16), nb)], tab, load_sem.at[tiles]
    )
    tab_load.start()
    q_load = pltpu.make_async_copy(
        quad.at[pl.ds(pl.multiple_of(b * nb, 16), nb)], q2.at[pl.ds(0, nb)], load_sem.at[tiles + 1]
    )
    q_load.start()

    barrier = pltpu.get_barrier_semaphore()
    pl.semaphore_signal(barrier, 1, device_id={"bin": sibling})
    for k in range(1, chips):
        pl.semaphore_signal(barrier, 1, device_id={"bin": far_to(k)})

    @pl.when(sp > 0)
    def _():
        pl.semaphore_signal(barrier, 1, device_id={"space": sp - 1})

    @pl.when(sp < s - 1)
    def _():
        pl.semaphore_signal(barrier, 1, device_id={"space": sp + 1})

    mask_f = mask[...].astype(jnp.float32)
    u_all = 0.77 * speed[...] * jnp.cos(heading[...])
    v_all = 0.77 * speed[...] * jnp.sin(heading[...])
    for r in range(rows):
        mask_s[HALO + r] = mask_f[r : r + 1]
        u_s[r] = u_all[r : r + 1]
        v_s[r] = v_all[r : r + 1]

    pl.semaphore_wait(barrier, chips + jnp.minimum(sp, 1) + jnp.minimum(s - 1 - sp, 1))

    up = {"space": sp + 1}
    down = {"space": sp - 1}
    to_up = [
        pltpu.make_async_remote_copy(
            spec.at[pl.ds(rows - HALO, HALO)], ext.at[pl.ds(0, HALO)],
            halo_send.at[0], halo_recv.at[0], device_id=up,
        ),
        pltpu.make_async_remote_copy(
            mask_s.at[pl.ds(rows, HALO)], mask_s.at[pl.ds(0, HALO)],
            halo_send.at[1], halo_recv.at[1], device_id=up,
        ),
    ]
    to_down = [
        pltpu.make_async_remote_copy(
            spec.at[pl.ds(0, HALO)], ext.at[pl.ds(rows + HALO, HALO)],
            halo_send.at[2], halo_recv.at[2], device_id=down,
        ),
        pltpu.make_async_remote_copy(
            mask_s.at[pl.ds(HALO, HALO)], mask_s.at[pl.ds(rows + HALO, HALO)],
            halo_send.at[3], halo_recv.at[3], device_id=down,
        ),
    ]

    @pl.when(sp < s - 1)
    def _():
        for copy in to_up:
            copy.start()

    @pl.when(sp > 0)
    def _():
        for copy in to_down:
            copy.start()

    @pl.when(sp == 0)
    def _():
        ext[pl.ds(0, HALO)] = jnp.zeros((HALO, nb, cols), jnp.float32)
        mask_s[pl.ds(0, HALO)] = jnp.zeros((HALO, 1, cols), jnp.float32)

    @pl.when(sp == s - 1)
    def _():
        ext[pl.ds(rows + HALO, HALO)] = jnp.zeros((HALO, nb, cols), jnp.float32)
        mask_s[pl.ds(rows + HALO, HALO)] = jnp.zeros((HALO, 1, cols), jnp.float32)

    def start_row(j):
        done = j * UNIT
        return lax.rem(done // TILE + 1, tiles) * TILE + lax.rem(done, TILE)

    def block(j, owner):
        return every.at[
            pl.ds(start_row(j), UNIT), pl.ds(pl.multiple_of(owner * nb, 16), nb)
        ]

    def far_copy(j, k, owner):
        part = block(j, owner)
        return pltpu.make_async_remote_copy(
            part, part, x_send.at[j, k], x_recv.at[j, k], device_id={"bin": far_to(k)}
        )

    def near_copy(j, k, owner):
        part = block(j, owner)
        return pltpu.make_async_remote_copy(
            part, part, f_send.at[j, k], f_recv.at[j, k], device_id={"bin": sibling}
        )

    def other(owner):
        return owner + 1 - 2 * core

    tab_load.wait()
    lane = lax.broadcasted_iota(jnp.int32, (8, cols), 1)

    def propagate(t):
        base = t * TILE

        def group(g, carry):
            at = pl.multiple_of(g * 8, 8)
            coef = tab[pl.ds(at, 8)]

            def wide(col):
                return jnp.broadcast_to(coef[:, col : col + 1], (8, cols))

            ax, ay = wide(AX), wide(AY)
            xpos, ypos = wide(XPOS) > 0.5, wide(YPOS) > 0.5
            edge = jnp.where(
                jnp.where(ypos, lane, cols - 1 - lane) == 0, 0.0, 1.0
            )
            field = [ext[base + m, pl.ds(at, 8)] for m in range(TILE + 2 * HALO)]
            for step in range(3):
                new = []
                for m in range(1, len(field) - 1):
                    e = field[m]
                    back = jnp.where(xpos, field[m - 1], field[m + 1])
                    side = edge * jnp.where(
                        ypos, pltpu.roll(e, 1, 1), pltpu.roll(e, cols - 1, 1)
                    )
                    value = e - ax * (e - back) - ay * (e - side)
                    new.append(value * mask_s[base + m + step])
                field = new
            where = pl.multiple_of(b * nb + at, 8)
            for m in range(TILE):
                every[base + m, pl.ds(where, 8)] = field[m]
            return carry

        lax.fori_loop(0, nb // 8, group, 0)

    def tile_step(i, carry):
        t = lax.rem(i + 1, tiles)

        @pl.when(i == 0)
        def _():
            for load in loads[:3]:
                load.wait()

        for later in range(3, tiles):

            @pl.when(i == later - 2)
            def _():
                loads[later].wait()

        @pl.when(i == tiles - 2)
        def _():
            @pl.when(sp > 0)
            def _():
                for copy in to_up:
                    copy.wait_recv()

            @pl.when(sp < s - 1)
            def _():
                for copy in to_down:
                    copy.wait_recv()

        propagate(t)

        def send(p, carry):
            j = i * (TILE // UNIT) + p
            for k in range(1, chips):
                far_copy(j, k, b).start()
            near_copy(j, 0, b).start()
            return carry

        lax.fori_loop(0, TILE // UNIT, send, 0)
        return carry

    lax.fori_loop(0, tiles, tile_step, 0)

    q_load.wait()
    turned = jnp.dot(
        reversal(nb, 0, nb, 0), q2[pl.ds(0, nb)], preferred_element_type=jnp.float32
    ).astype(jnp.bfloat16)
    for c in range(BINS // 256):
        q2[pl.ds(nb, nb), pl.ds(c * 256, 256)] = jnp.dot(
            turned, reversal(BINS, 0, 256, c * 256), preferred_element_type=jnp.float32
        ).astype(jnp.bfloat16)

    own = pl.ds(pl.multiple_of(b * nb, 16), nb)

    def compute(row):
        total = jnp.sum(every[row], axis=0, keepdims=True) * (1.0 / BINS)
        low = every[row].astype(jnp.bfloat16)
        coupled = jnp.dot(q2[...], low, preferred_element_type=jnp.float32)
        energy = every[row, own]
        along = tab[:, FCOS : FCOS + 1] * u_s[row] + tab[:, FSIN : FSIN + 1] * v_s[row]
        growth = GROWTH * jnp.maximum(along - 1.0, 0.0)
        rate = (
            growth
            + NONLINEAR * (coupled[:nb] + coupled[nb:])
            - DAMPING * tab[:, STEEP2 : STEEP2 + 1] * (total * total)
        )
        ext[HALO + row] = energy + TIME_STEP * (rate * energy)

    def out_copy(j):
        row = start_row(j)
        return pltpu.make_async_copy(
            ext.at[pl.ds(HALO + row, UNIT)], out.at[pl.ds(row, UNIT)], out_sem.at[j]
        )

    def unit_step(j, carry):
        @pl.when(j < units)
        def _():
            for k in range(1, chips):
                far_copy(j, k, far_from(k)).wait_recv()
                near_copy(j, k, far_from(k)).start()

        @pl.when(j > 0)
        def _():
            near_copy(j - 1, 0, sibling).wait_recv()
            for k in range(1, chips):
                near_copy(j - 1, k, other(far_from(k))).wait_recv()
            for r in range(UNIT):
                compute(start_row(j - 1) + r)
            out_copy(j - 1).start()

        return carry

    lax.fori_loop(0, units + 1, unit_step, 0)

    def drain(j, carry):
        for k in range(1, chips):
            far_copy(j, k, b).wait_send()
            near_copy(j, k, far_from(k)).wait_send()
        near_copy(j, 0, b).wait_send()
        out_copy(j).wait()
        return carry

    lax.fori_loop(0, units, drain, 0)

    @pl.when(sp < s - 1)
    def _():
        for copy in to_up:
            copy.wait_send()

    @pl.when(sp > 0)
    def _():
        for copy in to_down:
            copy.wait_send()


def on_device(n, s, spectrum, sea_mask, wind_speed, wind_heading, quad):
    nb, rows, cols = spectrum.shape
    units, chips, tiles = rows // UNIT, n // 2, rows // TILE
    vmem = pl.BlockSpec(memory_space=pltpu.VMEM)
    hbm = pl.BlockSpec(memory_space=pl.ANY)
    result = pl.pallas_call(
        functools.partial(kernel, n, s),
        out_shape=jax.ShapeDtypeStruct((rows, nb, cols), jnp.float32),
        in_specs=[hbm, vmem, vmem, vmem, hbm, hbm],
        out_specs=hbm,
        scratch_shapes=[
            pltpu.VMEM((rows + 2 * HALO, nb, cols), jnp.float32),
            pltpu.VMEM((rows + 2 * HALO, 1, cols), jnp.float32),
            pltpu.VMEM((rows, 1, cols), jnp.float32),
            pltpu.VMEM((rows, 1, cols), jnp.float32),
            pltpu.VMEM((rows, BINS, cols), jnp.float32),
            pltpu.VMEM((2 * nb, BINS), jnp.bfloat16),
            pltpu.VMEM((nb, 128), jnp.float32),
            pltpu.SemaphoreType.DMA((tiles + 2,)),
            pltpu.SemaphoreType.DMA((4,)),
            pltpu.SemaphoreType.DMA((4,)),
            pltpu.SemaphoreType.DMA((units, chips)),
            pltpu.SemaphoreType.DMA((units, chips)),
            pltpu.SemaphoreType.DMA((units, chips)),
            pltpu.SemaphoreType.DMA((units, chips)),
            pltpu.SemaphoreType.DMA((units,)),
        ],
        compiler_params=pltpu.CompilerParams(
            collective_id=0, has_side_effects=True, vmem_limit_bytes=60 * 1024 * 1024
        ),
        cost_estimate=pl.CostEstimate(
            flops=4 * nb * BINS * rows * cols, bytes_accessed=8 * nb * rows * cols, transcendentals=0
        ),
        name="wave_step",
    )(
        jnp.transpose(spectrum, (1, 0, 2)), sea_mask, wind_speed, wind_heading, quad,
        jnp.asarray(bin_tables()),
    )
    return jnp.transpose(result, (1, 0, 2))


def solution(mesh):
    return jax.shard_map(
        functools.partial(on_device, mesh.shape["bin"], mesh.shape["space"]),
        mesh=mesh,
        in_specs=(
            P("bin", "space", None),
            P("space", None),
            P("space", None),
            P("space", None),
            P(),
        ),
        out_specs=P("bin", "space", None),
        check_vma=False,
    )
```

time: 429 us -> 207 us (0.48)
  waiting for transfers between devices: 195 us -> 0 us
  Pallas kernels: 0 us -> 187 us
  local copies, waits for them, and re-layouts: 109 us -> 20 us
  other arithmetic: 83.2 us -> 0 us
  starting transfers between devices: 29.3 us -> 0 us
  matrix products: 8.72 us -> 0 us
    pallas_call x0 -> x1, Pallas kernels: none -> 187 us  [on_device(): pl.pallas_call(functools.partial(kernel, n, s), out_shape=jax.ShapeDtypeS...]
    all_to_all x2 -> x0, waiting for transfers between devices: 173 us -> none  [the longest x1 86.7 us: on_device(): lax.all_to_all(outgoing, 'bin', split_axis=1, concat_axis=0, tiled=True)]
    mul x6 -> x0, other arithmetic: 38.7 us -> none  [the longest x3 38.7 us: substep(): return updated * sea_rows]
    broadcast_in_dim x1 -> x0, local copies, waits for them, and re-layouts: 30.1 us -> none  [on_device(): sources(received[:, 0, :], quad, all_frequency)[:, None, :]]
    reshape x3 -> x0, local copies, waits for them, and re-layouts: 29.8 us -> none  [the longest x2 19.3 us: on_device(): outgoing = current.reshape(per_dev, groups, owned)]
    add x1 -> x0, other arithmetic: 26.8 us -> none  [on_device(): return current + TIME_STEP * (growth + source)]
    rev x2 -> x0, local copies, waits for them, and re-layouts: 26.1 us -> none  [reflect(): values.reshape(FREQS, DIRS, count)[:, ::-1].reshape(FREQS * DIRS, count)]
    ppermute x6 -> x0, waiting for transfers between devices: 21.7 us -> none  [the longest x3 17.9 us: extended(): lax.ppermute(lax.slice_in_dim(block, 0, width, axis=dim), axis, backward)]
  transfers between devices with their start and end apart: 8 -> 0, of which waited for: 8 -> 0; matrix products, arithmetic and copies ran while one was open for 0% -> 0% of each run, Pallas kernels for 0% -> 0%
where the time goes in v1:
time: 207 us
  Pallas kernels  187 us (90%)
  local copies, waits for them, and re-layouts  20 us (10%)
    pallas_call x1, Pallas kernels, on_device(): pl.pallas_call(functools.partial(kernel, n, s), out_shape=jax.ShapeDtypeS...  187 us
    transpose x1, local copies, waits for them, and re-layouts, on_device(): return jnp.transpose(result, (1, 0, 2))  11 us
    unnamed x1, local copies, waits for them, and re-layouts  8.98 us

profile of v1, /device:TPU:1, one launch (start us, length us, event | category | flops | bytes accessed | tf_op | source)
XLA Modules:
  0.0 207.1 jit_solution(2560081891439365774)
XLA Ops:
  0.0 9.0 %copy.10 = f32[192,40,256]{2,0,1:T(8,128)} copy(f32[192,40,256]{2,1,0:T(8,128)} %param.6) | data formatting | bytes 15728640 | tf_op args[0]
  9.0 187.1 %wave_step.1 = f32[40,192,256]{2,1,0:T(8,128)} custom-call(f32[40,192,256]{2,1,0:T(8,128)} %bitcast.5, s32[40,256]{1,0:T(8,128)} %mask.1, f32[40,256]{1,0:T(8,128)} %speed.1, f32[40,256]{1,0:T(8,128)} %heading.1, bf16[768,768]{1,0:T(8,128)(2,1)} %quad.1, f32[768,128]{1,0:T(8,128)} %constant.2.clone.table), custom_call_target="tpu_custom_call" | custom-call | flops 6039797760 | bytes 15728640 | tf_op jit(solution)/shard_map/wave_step/pallas_call | solution.py:338
  196.1 11.0 %copy.8 = f32[192,40,256]{2,1,0:T(8,128)} copy(f32[192,40,256]{2,0,1:T(8,128)} %bitcast.4) | data formatting | bytes 15728640 | tf_op jit(solution)/shard_map/transpose | solution.py:371

commit v2 on v1

--- a/solution.py
+++ b/solution.py
@@ -21,7 +21,8 @@
 GROWTH = 0.15
 
 HALO = 3
-TILE = 8
+CHUNK = 8
+TILE = 4
 UNIT = 2
 
 AX, AY, XPOS, YPOS, FCOS, FSIN, STEEP2 = range(7)
@@ -56,11 +57,12 @@
 
 def kernel(
     n, s, spec, mask, speed, heading, quad, table, out,
-    ext, mask_s, u_s, v_s, every, q2, tab,
+    nat, ext, mask_s, u_s, v_s, every, q2, tab,
     load_sem, halo_send, halo_recv, x_send, x_recv, f_send, f_recv, out_sem,
 ):
-    rows, nb, cols = spec.shape
+    nb, rows, cols = spec.shape
     tiles = rows // TILE
+    chunks = rows // CHUNK
     units = rows // UNIT
     chips = n // 2
     b = lax.axis_index("bin")
@@ -76,18 +78,18 @@
 
     loads = [
         pltpu.make_async_copy(
-            spec.at[pl.ds(t * TILE, TILE)], ext.at[pl.ds(HALO + t * TILE, TILE)], load_sem.at[t]
+            spec.at[:, pl.ds(c * CHUNK, CHUNK)], nat.at[c], load_sem.at[c]
         )
-        for t in range(tiles)
+        for c in range(chunks)
     ]
     for load in loads:
         load.start()
     tab_load = pltpu.make_async_copy(
-        table.at[pl.ds(pl.multiple_of(b * nb, 16), nb)], tab, load_sem.at[tiles]
+        table.at[pl.ds(pl.multiple_of(b * nb, 16), nb)], tab, load_sem.at[chunks]
     )
     tab_load.start()
     q_load = pltpu.make_async_copy(
-        quad.at[pl.ds(pl.multiple_of(b * nb, 16), nb)], q2.at[pl.ds(0, nb)], load_sem.at[tiles + 1]
+        quad.at[pl.ds(pl.multiple_of(b * nb, 16), nb)], q2.at[pl.ds(0, nb)], load_sem.at[chunks + 1]
     )
     q_load.start()
 
@@ -105,12 +107,28 @@
         pl.semaphore_signal(barrier, 1, device_id={"space": sp + 1})
 
     mask_f = mask[...].astype(jnp.float32)
-    u_all = 0.77 * speed[...] * jnp.cos(heading[...])
-    v_all = 0.77 * speed[...] * jnp.sin(heading[...])
     for r in range(rows):
         mask_s[HALO + r] = mask_f[r : r + 1]
-        u_s[r] = u_all[r : r + 1]
-        v_s[r] = v_all[r : r + 1]
+
+    def to_rows(c):
+        def group(g, carry):
+            at = pl.ds(pl.multiple_of(g * 8, 8), 8)
+            ext[pl.ds(HALO + c * CHUNK, CHUNK), at] = jnp.swapaxes(nat[c, at], 0, 1)
+            return carry
+
+        lax.fori_loop(0, nb // 8, group, 0)
+
+    def to_bins(c):
+        def group(g, carry):
+            at = pl.ds(pl.multiple_of(g * 8, 8), 8)
+            nat[c, at] = jnp.swapaxes(ext[pl.ds(HALO + c * CHUNK, CHUNK), at], 0, 1)
+            return carry
+
+        lax.fori_loop(0, nb // 8, group, 0)
+
+    for c in range(2):
+        loads[c].wait()
+        to_rows(c)
 
     pl.semaphore_wait(barrier, chips + jnp.minimum(sp, 1) + jnp.minimum(s - 1 - sp, 1))
 
@@ -118,7 +136,7 @@
     down = {"space": sp - 1}
     to_up = [
         pltpu.make_async_remote_copy(
-            spec.at[pl.ds(rows - HALO, HALO)], ext.at[pl.ds(0, HALO)],
+            ext.at[pl.ds(rows, HALO)], ext.at[pl.ds(0, HALO)],
             halo_send.at[0], halo_recv.at[0], device_id=up,
         ),
         pltpu.make_async_remote_copy(
@@ -128,7 +146,7 @@
     ]
     to_down = [
         pltpu.make_async_remote_copy(
-            spec.at[pl.ds(0, HALO)], ext.at[pl.ds(rows + HALO, HALO)],
+            ext.at[pl.ds(HALO, HALO)], ext.at[pl.ds(rows + HALO, HALO)],
             halo_send.at[2], halo_recv.at[2], device_id=down,
         ),
         pltpu.make_async_remote_copy(
@@ -137,11 +155,6 @@
         ),
     ]
 
-    @pl.when(sp < s - 1)
-    def _():
-        for copy in to_up:
-            copy.start()
-
     @pl.when(sp > 0)
     def _():
         for copy in to_down:
@@ -158,8 +171,7 @@
         mask_s[pl.ds(rows + HALO, HALO)] = jnp.zeros((HALO, 1, cols), jnp.float32)
 
     def start_row(j):
-        done = j * UNIT
-        return lax.rem(done // TILE + 1, tiles) * TILE + lax.rem(done, TILE)
+        return lax.rem(j * UNIT + CHUNK, rows)
 
     def block(j, owner):
         return every.at[
@@ -219,20 +231,23 @@
         lax.fori_loop(0, nb // 8, group, 0)
 
     def tile_step(i, carry):
-        t = lax.rem(i + 1, tiles)
-
-        @pl.when(i == 0)
+        t = lax.rem(i + CHUNK // TILE, tiles)
+
+        for c in range(2, chunks):
+
+            @pl.when(i == (c * CHUNK - HALO - CHUNK) // TILE)
+            def _():
+                loads[c].wait()
+                to_rows(c)
+
+        @pl.when(i == (rows - CHUNK - HALO - CHUNK) // TILE)
         def _():
-            for load in loads[:3]:
-                load.wait()
-
-        for later in range(3, tiles):
-
-            @pl.when(i == later - 2)
+            @pl.when(sp < s - 1)
             def _():
-                loads[later].wait()
-
-        @pl.when(i == tiles - 2)
+                for copy in to_up:
+                    copy.start()
+
+        @pl.when(i == (rows - HALO - CHUNK) // TILE)
         def _():
             @pl.when(sp > 0)
             def _():
@@ -257,6 +272,22 @@
         return carry
 
     lax.fori_loop(0, tiles, tile_step, 0)
+
+    @pl.when(sp < s - 1)
+    def _():
+        for copy in to_up:
+            copy.wait_send()
+
+    @pl.when(sp > 0)
+    def _():
+        for copy in to_down:
+            copy.wait_send()
+
+    u_all = 0.77 * speed[...] * jnp.cos(heading[...])
+    v_all = 0.77 * speed[...] * jnp.sin(heading[...])
+    for r in range(rows):
+        u_s[r] = u_all[r : r + 1]
+        v_s[r] = v_all[r : r + 1]
 
     q_load.wait()
     turned = jnp.dot(
@@ -283,10 +314,9 @@
         )
         ext[HALO + row] = energy + TIME_STEP * (rate * energy)
 
-    def out_copy(j):
-        row = start_row(j)
+    def out_copy(c):
         return pltpu.make_async_copy(
-            ext.at[pl.ds(HALO + row, UNIT)], out.at[pl.ds(row, UNIT)], out_sem.at[j]
+            nat.at[c], out.at[:, pl.ds(pl.multiple_of(c * CHUNK, CHUNK), CHUNK)], out_sem.at[c]
         )
 
     def unit_step(j, carry):
@@ -303,7 +333,12 @@
                 near_copy(j - 1, k, other(far_from(k))).wait_recv()
             for r in range(UNIT):
                 compute(start_row(j - 1) + r)
-            out_copy(j - 1).start()
+
+            @pl.when(lax.rem(j * UNIT, CHUNK) == 0)
+            def _():
+                c = start_row(j - 1) // CHUNK
+                to_bins(c)
+                out_copy(c).start()
 
         return carry
 
@@ -314,33 +349,25 @@
             far_copy(j, k, b).wait_send()
             near_copy(j, k, far_from(k)).wait_send()
         near_copy(j, 0, b).wait_send()
-        out_copy(j).wait()
         return carry
 
     lax.fori_loop(0, units, drain, 0)
-
-    @pl.when(sp < s - 1)
-    def _():
-        for copy in to_up:
-            copy.wait_send()
-
-    @pl.when(sp > 0)
-    def _():
-        for copy in to_down:
-            copy.wait_send()
+    for c in range(chunks):
+        out_copy(c).wait()
 
 
 def on_device(n, s, spectrum, sea_mask, wind_speed, wind_heading, quad):
     nb, rows, cols = spectrum.shape
-    units, chips, tiles = rows // UNIT, n // 2, rows // TILE
+    units, chips, chunks = rows // UNIT, n // 2, rows // CHUNK
     vmem = pl.BlockSpec(memory_space=pltpu.VMEM)
     hbm = pl.BlockSpec(memory_space=pl.ANY)
-    result = pl.pallas_call(
+    return pl.pallas_call(
         functools.partial(kernel, n, s),
-        out_shape=jax.ShapeDtypeStruct((rows, nb, cols), jnp.float32),
+        out_shape=jax.ShapeDtypeStruct((nb, rows, cols), jnp.float32),
         in_specs=[hbm, vmem, vmem, vmem, hbm, hbm],
         out_specs=hbm,
         scratch_shapes=[
+            pltpu.VMEM((chunks, nb, CHUNK, cols), jnp.float32),
             pltpu.VMEM((rows + 2 * HALO, nb, cols), jnp.float32),
             pltpu.VMEM((rows + 2 * HALO, 1, cols), jnp.float32),
             pltpu.VMEM((rows, 1, cols), jnp.float32),
@@ -348,27 +375,25 @@
             pltpu.VMEM((rows, BINS, cols), jnp.float32),
             pltpu.VMEM((2 * nb, BINS), jnp.bfloat16),
             pltpu.VMEM((nb, 128), jnp.float32),
-            pltpu.SemaphoreType.DMA((tiles + 2,)),
+            pltpu.SemaphoreType.DMA((chunks + 2,)),
             pltpu.SemaphoreType.DMA((4,)),
             pltpu.SemaphoreType.DMA((4,)),
             pltpu.SemaphoreType.DMA((units, chips)),
             pltpu.SemaphoreType.DMA((units, chips)),
             pltpu.SemaphoreType.DMA((units, chips)),
             pltpu.SemaphoreType.DMA((units, chips)),
-            pltpu.SemaphoreType.DMA((units,)),
+            pltpu.SemaphoreType.DMA((chunks,)),
         ],
         compiler_params=pltpu.CompilerParams(
-            collective_id=0, has_side_effects=True, vmem_limit_bytes=60 * 1024 * 1024
+            collective_id=0, has_side_effects=True, vmem_limit_bytes=53 * 1024 * 1024
         ),
         cost_estimate=pl.CostEstimate(
             flops=4 * nb * BINS * rows * cols, bytes_accessed=8 * nb * rows * cols, transcendentals=0
         ),
         name="wave_step",
     )(
-        jnp.transpose(spectrum, (1, 0, 2)), sea_mask, wind_speed, wind_heading, quad,
-        jnp.asarray(bin_tables()),
+        spectrum, sea_mask, wind_speed, wind_heading, quad, jnp.asarray(bin_tables()),
     )
-    return jnp.transpose(result, (1, 0, 2))
 
 
 def solution(mesh):

time: 207 us -> 197 us (0.952)
  local copies, waits for them, and re-layouts: 20 us -> 10.3 us
    transpose x1 -> x0, local copies, waits for them, and re-layouts: 11 us -> none  [on_device(): return jnp.transpose(result, (1, 0, 2))]
    unnamed x1 -> x9, local copies, waits for them, and re-layouts: 8.98 us -> 10.3 us
where the time goes in v2:
time: 197 us; the launch traced here: 196 us
  Pallas kernels  186 us (94%)
  local copies, waits for them, and re-layouts  10.3 us (5%)
    pallas_call x1, Pallas kernels, on_device(): pl.pallas_call(functools.partial(kernel, n, s), out_shape=jax.ShapeDtypeS...  186 us
    unnamed x9, local copies, waits for them, and re-layouts  10.3 us

profile of v2, /device:TPU:1, one launch (start us, length us, event | category | flops | bytes accessed | tf_op | source)
XLA Modules:
  0.0 196.2 jit_solution(1752973326962872818)
XLA Ops:
  0.0 0.0 copy-start
  0.0 0.8 copy-done
  0.8 0.0 copy-start.1
  0.8 0.8 copy-done.1
  1.6 0.0 copy-start.2
  1.6 0.8 copy-done.2
  2.3 0.0 copy-start.3
  2.3 1.0 copy-done.3
  3.3 185.9 %wave_step.1 = f32[192,40,256]{2,1,0:T(8,128)} custom-call(f32[192,40,256]{2,1,0:T(8,128)} %spec.1, s32[40,256]{1,0:T(8,128)S(1)} %copy-done, f32[40,256]{1,0:T(8,128)S(1)} %copy-done.1, f32[40,256]{1,0:T(8,128)S(1)} %copy-done.2, bf16[768,768]{1,0:T(8,128)(2,1)} %quad.1, f32[768,128]{1,0:T(8,128)S(1)} %copy-done.3), custom_call_target="tpu_custom_call" | custom-call | flops 6039797760 | bytes 15728640 | tf_op jit(solution)/shard_map/wave_step/pallas_call | solution.py:364
  189.3 7.0 %copy.8 = f32[192,40,256]{2,1,0:T(8,128)} copy(f32[192,40,256]{2,1,0:T(8,128)} %wave_step.1) | data formatting | bytes 15728640
Async XLA Ops:
  0.0 0.8 copy-start
  0.8 0.8 copy-start.1
  1.6 0.8 copy-start.2
  2.3 1.0 copy-start.3

commit v3 on v2

--- a/solution.py
+++ b/solution.py
@@ -22,7 +22,7 @@
 
 HALO = 3
 CHUNK = 8
-TILE = 4
+TILE = 2
 UNIT = 2
 
 AX, AY, XPOS, YPOS, FCOS, FSIN, STEEP2 = range(7)
@@ -56,9 +56,9 @@
 
 
 def kernel(
-    n, s, spec, mask, speed, heading, quad, table, out,
-    nat, ext, mask_s, u_s, v_s, every, q2, tab,
-    load_sem, halo_send, halo_recv, x_send, x_recv, f_send, f_recv, out_sem,
+    n, s, spec, mask_h, speed_h, heading_h, quad, table, nat,
+    mask, speed, heading, ext, mask_s, u_s, v_s, every, q2, tab,
+    load_sem, small_sem, halo_send, halo_recv, x_send, x_recv, f_send, f_recv,
 ):
     nb, rows, cols = spec.shape
     tiles = rows // TILE
@@ -78,12 +78,23 @@
 
     loads = [
         pltpu.make_async_copy(
-            spec.at[:, pl.ds(c * CHUNK, CHUNK)], nat.at[c], load_sem.at[c]
+            spec.at[:, pl.ds(c * CHUNK, CHUNK)], nat.at[:, pl.ds(c * CHUNK, CHUNK)],
+            load_sem.at[c],
         )
         for c in range(chunks)
     ]
-    for load in loads:
+    smalls = [
+        pltpu.make_async_copy(source, target, small_sem.at[at])
+        for at, (source, target) in enumerate(
+            ((mask_h, mask), (speed_h, speed), (heading_h, heading))
+        )
+    ]
+    loads[0].start()
+    smalls[0].start()
+    for load in loads[1:]:
         load.start()
+    for small in smalls[1:]:
+        small.start()
     tab_load = pltpu.make_async_copy(
         table.at[pl.ds(pl.multiple_of(b * nb, 16), nb)], tab, load_sem.at[chunks]
     )
@@ -106,6 +117,7 @@
     def _():
         pl.semaphore_signal(barrier, 1, device_id={"space": sp + 1})
 
+    smalls[0].wait()
     mask_f = mask[...].astype(jnp.float32)
     for r in range(rows):
         mask_s[HALO + r] = mask_f[r : r + 1]
@@ -113,7 +125,9 @@
     def to_rows(c):
         def group(g, carry):
             at = pl.ds(pl.multiple_of(g * 8, 8), 8)
-            ext[pl.ds(HALO + c * CHUNK, CHUNK), at] = jnp.swapaxes(nat[c, at], 0, 1)
+            ext[pl.ds(HALO + c * CHUNK, CHUNK), at] = jnp.swapaxes(
+                nat[at, pl.ds(c * CHUNK, CHUNK)], 0, 1
+            )
             return carry
 
         lax.fori_loop(0, nb // 8, group, 0)
@@ -121,7 +135,9 @@
     def to_bins(c):
         def group(g, carry):
             at = pl.ds(pl.multiple_of(g * 8, 8), 8)
-            nat[c, at] = jnp.swapaxes(ext[pl.ds(HALO + c * CHUNK, CHUNK), at], 0, 1)
+            nat[at, pl.ds(pl.multiple_of(c * CHUNK, CHUNK), CHUNK)] = jnp.swapaxes(
+                ext[pl.ds(HALO + c * CHUNK, CHUNK), at], 0, 1
+            )
             return carry
 
         lax.fori_loop(0, nb // 8, group, 0)
@@ -283,6 +299,8 @@
         for copy in to_down:
             copy.wait_send()
 
+    for small in smalls[1:]:
+        small.wait()
     u_all = 0.77 * speed[...] * jnp.cos(heading[...])
     v_all = 0.77 * speed[...] * jnp.sin(heading[...])
     for r in range(rows):
@@ -314,11 +332,6 @@
         )
         ext[HALO + row] = energy + TIME_STEP * (rate * energy)
 
-    def out_copy(c):
-        return pltpu.make_async_copy(
-            nat.at[c], out.at[:, pl.ds(pl.multiple_of(c * CHUNK, CHUNK), CHUNK)], out_sem.at[c]
-        )
-
     def unit_step(j, carry):
         @pl.when(j < units)
         def _():
@@ -336,9 +349,7 @@
 
             @pl.when(lax.rem(j * UNIT, CHUNK) == 0)
             def _():
-                c = start_row(j - 1) // CHUNK
-                to_bins(c)
-                out_copy(c).start()
+                to_bins(start_row(j - 1) // CHUNK)
 
         return carry
 
@@ -352,8 +363,6 @@
         return carry
 
     lax.fori_loop(0, units, drain, 0)
-    for c in range(chunks):
-        out_copy(c).wait()
 
 
 def on_device(n, s, spectrum, sea_mask, wind_speed, wind_heading, quad):
@@ -363,11 +372,13 @@
     hbm = pl.BlockSpec(memory_space=pl.ANY)
     return pl.pallas_call(
         functools.partial(kernel, n, s),
-        out_shape=jax.ShapeDtypeStruct((nb, rows, cols), jnp.float32),
-        in_specs=[hbm, vmem, vmem, vmem, hbm, hbm],
-        out_specs=hbm,
+        out_shape=pltpu.VMEM((nb, rows, cols), jnp.float32),
+        in_specs=[hbm] * 6,
+        out_specs=vmem,
         scratch_shapes=[
-            pltpu.VMEM((chunks, nb, CHUNK, cols), jnp.float32),
+            pltpu.VMEM((rows, cols), jnp.int32),
+            pltpu.VMEM((rows, cols), jnp.float32),
+            pltpu.VMEM((rows, cols), jnp.float32),
             pltpu.VMEM((rows + 2 * HALO, nb, cols), jnp.float32),
             pltpu.VMEM((rows + 2 * HALO, 1, cols), jnp.float32),
             pltpu.VMEM((rows, 1, cols), jnp.float32),
@@ -376,16 +387,16 @@
             pltpu.VMEM((2 * nb, BINS), jnp.bfloat16),
             pltpu.VMEM((nb, 128), jnp.float32),
             pltpu.SemaphoreType.DMA((chunks + 2,)),
+            pltpu.SemaphoreType.DMA((3,)),
             pltpu.SemaphoreType.DMA((4,)),
             pltpu.SemaphoreType.DMA((4,)),
             pltpu.SemaphoreType.DMA((units, chips)),
             pltpu.SemaphoreType.DMA((units, chips)),
             pltpu.SemaphoreType.DMA((units, chips)),
             pltpu.SemaphoreType.DMA((units, chips)),
-            pltpu.SemaphoreType.DMA((chunks,)),
         ],
         compiler_params=pltpu.CompilerParams(
-            collective_id=0, has_side_effects=True, vmem_limit_bytes=53 * 1024 * 1024
+            collective_id=0, has_side_effects=True, vmem_limit_bytes=56 * 1024 * 1024
         ),
         cost_estimate=pl.CostEstimate(
             flops=4 * nb * BINS * rows * cols, bytes_accessed=8 * nb * rows * cols, transcendentals=0

time: 197 us -> 189 us (0.959)
  local copies, waits for them, and re-layouts: 10.3 us -> 3.22 us
    unnamed x9 -> x1, local copies, waits for them, and re-layouts: 10.3 us -> 3.22 us
where the time goes in v3:
time: 189 us
  Pallas kernels  186 us (98%)
  local copies, waits for them, and re-layouts  3.22 us (2%)
    pallas_call x1, Pallas kernels, on_device(): pl.pallas_call(functools.partial(kernel, n, s), out_shape=pltpu.VMEM((nb,...  186 us

profile of v3, /device:TPU:1, one launch (start us, length us, event | category | flops | bytes accessed | tf_op | source)
XLA Modules:
  0.0 188.9 jit_solution(17742683351185105463)
XLA Ops:
  0.0 185.6 %wave_step.1 = f32[192,40,256]{2,1,0:T(8,128)S(1)} custom-call(f32[192,40,256]{2,1,0:T(8,128)} %spec.1, s32[40,256]{1,0:T(8,128)} %mask_h.1, f32[40,256]{1,0:T(8,128)} %speed_h.1, f32[40,256]{1,0:T(8,128)} %heading_h.1, bf16[768,768]{1,0:T(8,128)(2,1)} %quad.1, f32[768,128]{1,0:T(8,128)} %constant.2.clone.table), custom_call_target="tpu_custom_call" | custom-call | flops 6039797760 | bytes 15728640 | tf_op jit(solution)/shard_map/wave_step/pallas_call | solution.py:373
  185.7 3.2 %copy.8 = f32[192,40,256]{2,1,0:T(8,128)} copy(f32[192,40,256]{2,1,0:T(8,128)S(1)} %wave_step.1) | data formatting | bytes 15728640

commit v4 on v3

--- a/solution.py
+++ b/solution.py
@@ -55,14 +55,20 @@
     return jnp.where(i + j == 2 * DIRS * level + (DIRS - 1), 1.0, 0.0).astype(jnp.bfloat16)
 
 
+def part_count(nb):
+    return 4 if nb % 32 == 0 else 2
+
+
 def kernel(
     n, s, spec, mask_h, speed_h, heading_h, quad, table, nat,
     mask, speed, heading, ext, mask_s, u_s, v_s, every, q2, tab,
-    load_sem, small_sem, halo_send, halo_recv, x_send, x_recv, f_send, f_recv,
+    load_sem, first_sem, small_sem, halo_send, halo_recv, x_send, x_recv, f_send, f_recv, part_send, part_recv,
 ):
     nb, rows, cols = spec.shape
     tiles = rows // TILE
     chunks = rows // CHUNK
+    parts = part_count(nb)
+    width = nb // parts
     units = rows // UNIT
     chips = n // 2
     b = lax.axis_index("bin")
@@ -81,7 +87,15 @@
             spec.at[:, pl.ds(c * CHUNK, CHUNK)], nat.at[:, pl.ds(c * CHUNK, CHUNK)],
             load_sem.at[c],
         )
-        for c in range(chunks)
+        for c in range(2, chunks)
+    ]
+    firsts = [
+        pltpu.make_async_copy(
+            spec.at[pl.ds(q * width, width), pl.ds(0, 2 * CHUNK)],
+            nat.at[pl.ds(q * width, width), pl.ds(0, 2 * CHUNK)],
+            first_sem.at[q],
+        )
+        for q in range(parts)
     ]
     smalls = [
         pltpu.make_async_copy(source, target, small_sem.at[at])
@@ -89,16 +103,16 @@
             ((mask_h, mask), (speed_h, speed), (heading_h, heading))
         )
     ]
-    loads[0].start()
+    firsts[0].start()
     smalls[0].start()
-    for load in loads[1:]:
-        load.start()
     for small in smalls[1:]:
         small.start()
     tab_load = pltpu.make_async_copy(
         table.at[pl.ds(pl.multiple_of(b * nb, 16), nb)], tab, load_sem.at[chunks]
     )
     tab_load.start()
+    for load in firsts[1:] + loads:
+        load.start()
     q_load = pltpu.make_async_copy(
         quad.at[pl.ds(pl.multiple_of(b * nb, 16), nb)], q2.at[pl.ds(0, nb)], load_sem.at[chunks + 1]
     )
@@ -122,7 +136,7 @@
     for r in range(rows):
         mask_s[HALO + r] = mask_f[r : r + 1]
 
-    def to_rows(c):
+    def to_rows(c, first=0, last=nb // 8):
         def group(g, carry):
             at = pl.ds(pl.multiple_of(g * 8, 8), 8)
             ext[pl.ds(HALO + c * CHUNK, CHUNK), at] = jnp.swapaxes(
@@ -130,7 +144,7 @@
             )
             return carry
 
-        lax.fori_loop(0, nb // 8, group, 0)
+        lax.fori_loop(first, last, group, 0)
 
     def to_bins(c):
         def group(g, carry):
@@ -142,12 +156,6 @@
 
         lax.fori_loop(0, nb // 8, group, 0)
 
-    for c in range(2):
-        loads[c].wait()
-        to_rows(c)
-
-    pl.semaphore_wait(barrier, chips + jnp.minimum(sp, 1) + jnp.minimum(s - 1 - sp, 1))
-
     up = {"space": sp + 1}
     down = {"space": sp - 1}
     to_up = [
@@ -171,48 +179,54 @@
         ),
     ]
 
-    @pl.when(sp > 0)
-    def _():
-        for copy in to_down:
-            copy.start()
-
-    @pl.when(sp == 0)
-    def _():
-        ext[pl.ds(0, HALO)] = jnp.zeros((HALO, nb, cols), jnp.float32)
-        mask_s[pl.ds(0, HALO)] = jnp.zeros((HALO, 1, cols), jnp.float32)
-
-    @pl.when(sp == s - 1)
-    def _():
-        ext[pl.ds(rows + HALO, HALO)] = jnp.zeros((HALO, nb, cols), jnp.float32)
-        mask_s[pl.ds(rows + HALO, HALO)] = jnp.zeros((HALO, 1, cols), jnp.float32)
-
     def start_row(j):
         return lax.rem(j * UNIT + CHUNK, rows)
 
-    def block(j, owner):
-        return every.at[
-            pl.ds(start_row(j), UNIT), pl.ds(pl.multiple_of(owner * nb, 16), nb)
-        ]
-
-    def far_copy(j, k, owner):
-        part = block(j, owner)
+    last = units - 1
+    last_row = (last * UNIT + CHUNK) % rows
+
+    def block(row, count, owner):
+        return every.at[pl.ds(row, count), pl.ds(pl.multiple_of(owner * nb, 16), nb)]
+
+    def far_piece(row, count, j, k, owner):
+        part = block(row, count, owner)
         return pltpu.make_async_remote_copy(
             part, part, x_send.at[j, k], x_recv.at[j, k], device_id={"bin": far_to(k)}
         )
 
-    def near_copy(j, k, owner):
-        part = block(j, owner)
+    def near_piece(row, count, j, k, owner):
+        part = block(row, count, owner)
         return pltpu.make_async_remote_copy(
             part, part, f_send.at[j, k], f_recv.at[j, k], device_id={"bin": sibling}
         )
 
+    def far_copy(j, k, owner):
+        return far_piece(start_row(j), UNIT, j, k, owner)
+
+    def near_copy(j, k, owner):
+        return near_piece(start_row(j), UNIT, j, k, owner)
+
+    def far_last(r, k, owner):
+        return far_piece(last_row + r, 1, last + r, k, owner)
+
+    def near_last(r, k, owner):
+        return near_piece(last_row + r, 1, last + r, k, owner)
+
+    def far_part(q, k, owner):
+        part = every.at[
+            pl.ds(CHUNK, UNIT), pl.ds(pl.multiple_of(owner * nb + q * width, 8), width)
+        ]
+        return pltpu.make_async_remote_copy(
+            part, part, part_send.at[q, k], part_recv.at[q, k], device_id={"bin": far_to(k)}
+        )
+
     def other(owner):
         return owner + 1 - 2 * core
 
     tab_load.wait()
     lane = lax.broadcasted_iota(jnp.int32, (8, cols), 1)
 
-    def propagate(t):
+    def propagate(t, first=0, last=nb // 8):
         base = t * TILE
 
         def group(g, carry):
@@ -244,7 +258,34 @@
                 every[base + m, pl.ds(where, 8)] = field[m]
             return carry
 
-        lax.fori_loop(0, nb // 8, group, 0)
+        lax.fori_loop(first, last, group, 0)
+
+    for q in range(parts):
+        span = (q * width // 8, (q + 1) * width // 8)
+        firsts[q].wait()
+        for c in range(2):
+            to_rows(c, *span)
+        propagate(CHUNK // TILE, *span)
+        if q == 0:
+            pl.semaphore_wait(barrier, chips + jnp.minimum(sp, 1) + jnp.minimum(s - 1 - sp, 1))
+        for k in range(1, chips):
+            far_part(q, k, b).start()
+    near_copy(0, 0, b).start()
+
+    @pl.when(sp > 0)
+    def _():
+        for copy in to_down:
+            copy.start()
+
+    @pl.when(sp == 0)
+    def _():
+        ext[pl.ds(0, HALO)] = jnp.zeros((HALO, nb, cols), jnp.float32)
+        mask_s[pl.ds(0, HALO)] = jnp.zeros((HALO, 1, cols), jnp.float32)
+
+    @pl.when(sp == s - 1)
+    def _():
+        ext[pl.ds(rows + HALO, HALO)] = jnp.zeros((HALO, nb, cols), jnp.float32)
+        mask_s[pl.ds(rows + HALO, HALO)] = jnp.zeros((HALO, 1, cols), jnp.float32)
 
     def tile_step(i, carry):
         t = lax.rem(i + CHUNK // TILE, tiles)
@@ -253,7 +294,7 @@
 
             @pl.when(i == (c * CHUNK - HALO - CHUNK) // TILE)
             def _():
-                loads[c].wait()
+                loads[c - 2].wait()
                 to_rows(c)
 
         @pl.when(i == (rows - CHUNK - HALO - CHUNK) // TILE)
@@ -277,17 +318,22 @@
 
         propagate(t)
 
-        def send(p, carry):
-            j = i * (TILE // UNIT) + p
+        @pl.when(i < last)
+        def _():
             for k in range(1, chips):
-                far_copy(j, k, b).start()
-            near_copy(j, 0, b).start()
-            return carry
-
-        lax.fori_loop(0, TILE // UNIT, send, 0)
+                far_copy(i, k, b).start()
+            near_copy(i, 0, b).start()
+
+        @pl.when(i == last)
+        def _():
+            for r in range(UNIT):
+                for k in range(1, chips):
+                    far_last(r, k, b).start()
+                near_last(r, 0, b).start()
+
         return carry
 
-    lax.fori_loop(0, tiles, tile_step, 0)
+    lax.fori_loop(1, tiles, tile_step, 0)
 
     @pl.when(sp < s - 1)
     def _():
@@ -333,36 +379,63 @@
         ext[HALO + row] = energy + TIME_STEP * (rate * energy)
 
     def unit_step(j, carry):
-        @pl.when(j < units)
+        @pl.when(j == 0)
+        def _():
+            for k in range(1, chips):
+                for q in range(parts):
+                    far_part(q, k, far_from(k)).wait_recv()
+                near_copy(j, k, far_from(k)).start()
+
+        @pl.when(j > 0)
         def _():
             for k in range(1, chips):
                 far_copy(j, k, far_from(k)).wait_recv()
                 near_copy(j, k, far_from(k)).start()
 
+        near_copy(j, 0, sibling).wait_recv()
+        for k in range(1, chips):
+            near_copy(j, k, other(far_from(k))).wait_recv()
+        for r in range(UNIT):
+            compute(start_row(j) + r)
+
+        @pl.when(lax.rem((j + 1) * UNIT, CHUNK) == 0)
+        def _():
+            to_bins(start_row(j) // CHUNK)
+
+        return carry
+
+    lax.fori_loop(0, last, unit_step, 0)
+
+    for r in range(UNIT):
+        for k in range(1, chips):
+            far_last(r, k, far_from(k)).wait_recv()
+            near_last(r, k, far_from(k)).start()
+        near_last(r, 0, sibling).wait_recv()
+        for k in range(1, chips):
+            near_last(r, k, other(far_from(k))).wait_recv()
+        compute(last_row + r)
+    to_bins(last_row // CHUNK)
+
+    def drain(j, carry):
         @pl.when(j > 0)
         def _():
-            near_copy(j - 1, 0, sibling).wait_recv()
             for k in range(1, chips):
-                near_copy(j - 1, k, other(far_from(k))).wait_recv()
-            for r in range(UNIT):
-                compute(start_row(j - 1) + r)
-
-            @pl.when(lax.rem(j * UNIT, CHUNK) == 0)
-            def _():
-                to_bins(start_row(j - 1) // CHUNK)
-
-        return carry
-
-    lax.fori_loop(0, units + 1, unit_step, 0)
-
-    def drain(j, carry):
-        for k in range(1, chips):
-            far_copy(j, k, b).wait_send()
+                far_copy(j, k, b).wait_send()
+
+        for k in range(1, chips):
             near_copy(j, k, far_from(k)).wait_send()
         near_copy(j, 0, b).wait_send()
         return carry
 
-    lax.fori_loop(0, units, drain, 0)
+    lax.fori_loop(0, last, drain, 0)
+    for r in range(UNIT):
+        for k in range(1, chips):
+            far_last(r, k, b).wait_send()
+            near_last(r, k, far_from(k)).wait_send()
+        near_last(r, 0, b).wait_send()
+    for q in range(parts):
+        for k in range(1, chips):
+            far_part(q, k, b).wait_send()
 
 
 def on_device(n, s, spectrum, sea_mask, wind_speed, wind_heading, quad):
@@ -387,13 +460,16 @@
             pltpu.VMEM((2 * nb, BINS), jnp.bfloat16),
             pltpu.VMEM((nb, 128), jnp.float32),
             pltpu.SemaphoreType.DMA((chunks + 2,)),
+            pltpu.SemaphoreType.DMA((part_count(nb),)),
             pltpu.SemaphoreType.DMA((3,)),
             pltpu.SemaphoreType.DMA((4,)),
             pltpu.SemaphoreType.DMA((4,)),
-            pltpu.SemaphoreType.DMA((units, chips)),
-            pltpu.SemaphoreType.DMA((units, chips)),
-            pltpu.SemaphoreType.DMA((units, chips)),
-            pltpu.SemaphoreType.DMA((units, chips)),
+            pltpu.SemaphoreType.DMA((units - 1 + UNIT, chips)),
+            pltpu.SemaphoreType.DMA((units - 1 + UNIT, chips)),
+            pltpu.SemaphoreType.DMA((units - 1 + UNIT, chips)),
+            pltpu.SemaphoreType.DMA((units - 1 + UNIT, chips)),
+            pltpu.SemaphoreType.DMA((part_count(nb), chips)),
+            pltpu.SemaphoreType.DMA((part_count(nb), chips)),
         ],
         compiler_params=pltpu.CompilerParams(
             collective_id=0, has_side_effects=True, vmem_limit_bytes=56 * 1024 * 1024

time: 189 us -> 186 us (0.984)
  Pallas kernels: 186 us -> 183 us
    pallas_call x1, Pallas kernels: 186 us -> 183 us  [on_device(): pl.pallas_call(functools.partial(kernel, n, s), out_shape=pltpu.VMEM((nb,...]
where the time goes in v4:
time: 186 us
  Pallas kernels  183 us (98%)
  local copies, waits for them, and re-layouts  3.22 us (2%)
    pallas_call x1, Pallas kernels, on_device(): pl.pallas_call(functools.partial(kernel, n, s), out_shape=pltpu.VMEM((nb,...  183 us

profile of v4, /device:TPU:1, one launch (start us, length us, event | category | flops | bytes accessed | tf_op | source)
XLA Modules:
  0.0 185.7 jit_solution(8857862321725054295)
XLA Ops:
  0.0 182.5 %wave_step.1 = f32[192,40,256]{2,1,0:T(8,128)S(1)} custom-call(f32[192,40,256]{2,1,0:T(8,128)} %spec.1, s32[40,256]{1,0:T(8,128)} %mask_h.1, f32[40,256]{1,0:T(8,128)} %speed_h.1, f32[40,256]{1,0:T(8,128)} %heading_h.1, bf16[768,768]{1,0:T(8,128)(2,1)} %quad.1, f32[768,128]{1,0:T(8,128)} %constant.2.clone.table), custom_call_target="tpu_custom_call" | custom-call | flops 6039797760 | bytes 15728640 | tf_op jit(solution)/shard_map/wave_step/pallas_call | solution.py:446
  182.5 3.2 %copy.8 = f32[192,40,256]{2,1,0:T(8,128)} copy(f32[192,40,256]{2,1,0:T(8,128)S(1)} %wave_step.1) | data formatting | bytes 15728640

commit v5 on v4

--- a/solution.py
+++ b/solution.py
@@ -202,6 +202,15 @@
 
     def far_copy(j, k, owner):
         return far_piece(start_row(j), UNIT, j, k, owner)
+
+    def far_pair(j, k, owner):
+        return far_piece(start_row(j), 2 * UNIT, j, k, owner)
+
+    def alone(j):
+        return (j == 1) | (j == last - 1)
+
+    def paired(j):
+        return (j > 1) & (j < last - 1) & (lax.rem(j, 2) == 0)
 
     def near_copy(j, k, owner):
         return near_piece(start_row(j), UNIT, j, k, owner)
@@ -318,10 +327,18 @@
 
         propagate(t)
 
+        @pl.when(alone(i))
+        def _():
+            for k in range(1, chips):
+                far_copy(i, k, b).start()
+
+        @pl.when(paired(i - 1))
+        def _():
+            for k in range(1, chips):
+                far_pair(i - 1, k, b).start()
+
         @pl.when(i < last)
         def _():
-            for k in range(1, chips):
-                far_copy(i, k, b).start()
             near_copy(i, 0, b).start()
 
         @pl.when(i == last)
@@ -384,14 +401,19 @@
             for k in range(1, chips):
                 for q in range(parts):
                     far_part(q, k, far_from(k)).wait_recv()
-                near_copy(j, k, far_from(k)).start()
-
-        @pl.when(j > 0)
+
+        @pl.when(alone(j))
         def _():
             for k in range(1, chips):
                 far_copy(j, k, far_from(k)).wait_recv()
-                near_copy(j, k, far_from(k)).start()
-
+
+        @pl.when(paired(j))
+        def _():
+            for k in range(1, chips):
+                far_pair(j, k, far_from(k)).wait_recv()
+
+        for k in range(1, chips):
+            near_copy(j, k, far_from(k)).start()
         near_copy(j, 0, sibling).wait_recv()
         for k in range(1, chips):
             near_copy(j, k, other(far_from(k))).wait_recv()
@@ -417,10 +439,15 @@
     to_bins(last_row // CHUNK)
 
     def drain(j, carry):
-        @pl.when(j > 0)
+        @pl.when(alone(j))
         def _():
             for k in range(1, chips):
                 far_copy(j, k, b).wait_send()
+
+        @pl.when(paired(j))
+        def _():
+            for k in range(1, chips):
+                far_pair(j, k, b).wait_send()
 
         for k in range(1, chips):
             near_copy(j, k, far_from(k)).wait_send()

time: 186 us -> 190 us (1.022)
  Pallas kernels: 183 us -> 186 us
    pallas_call x1, Pallas kernels: 183 us -> 186 us  [on_device(): pl.pallas_call(functools.partial(kernel, n, s), out_shape=pltpu.VMEM((nb,...]
where the time goes in v5:
time: 190 us
  Pallas kernels  186 us (98%)
  local copies, waits for them, and re-layouts  3.22 us (2%)
    pallas_call x1, Pallas kernels, on_device(): pl.pallas_call(functools.partial(kernel, n, s), out_shape=pltpu.VMEM((nb,...  186 us

profile of v5, /device:TPU:1, one launch (start us, length us, event | category | flops | bytes accessed | tf_op | source)
XLA Modules:
  0.0 189.6 jit_solution(13810441613410651231)
XLA Ops:
  0.0 186.4 %wave_step.1 = f32[192,40,256]{2,1,0:T(8,128)S(1)} custom-call(f32[192,40,256]{2,1,0:T(8,128)} %spec.1, s32[40,256]{1,0:T(8,128)} %mask_h.1, f32[40,256]{1,0:T(8,128)} %speed_h.1, f32[40,256]{1,0:T(8,128)} %heading_h.1, bf16[768,768]{1,0:T(8,128)(2,1)} %quad.1, f32[768,128]{1,0:T(8,128)} %constant.2.clone.table), custom_call_target="tpu_custom_call" | custom-call | flops 6039797760 | bytes 15728640 | tf_op jit(solution)/shard_map/wave_step/pallas_call | solution.py:473
  186.4 3.2 %copy.8 = f32[192,40,256]{2,1,0:T(8,128)} copy(f32[192,40,256]{2,1,0:T(8,128)S(1)} %wave_step.1) | data formatting | bytes 15728640

commit v6 on v4

--- a/solution.py
+++ b/solution.py
@@ -183,6 +183,7 @@
         return lax.rem(j * UNIT + CHUNK, rows)
 
     last = units - 1
+    ahead = units // 2
     last_row = (last * UNIT + CHUNK) % rows
 
     def block(row, count, owner):
@@ -318,17 +319,18 @@
 
         propagate(t)
 
-        @pl.when(i < last)
+        @pl.when(i < ahead)
         def _():
             for k in range(1, chips):
                 far_copy(i, k, b).start()
+
+        @pl.when(i < last)
+        def _():
             near_copy(i, 0, b).start()
 
         @pl.when(i == last)
         def _():
             for r in range(UNIT):
-                for k in range(1, chips):
-                    far_last(r, k, b).start()
                 near_last(r, 0, b).start()
 
         return carry
@@ -391,6 +393,17 @@
             for k in range(1, chips):
                 far_copy(j, k, far_from(k)).wait_recv()
                 near_copy(j, k, far_from(k)).start()
+
+        @pl.when(j + ahead < last)
+        def _():
+            for k in range(1, chips):
+                far_copy(j + ahead, k, b).start()
+
+        @pl.when(j + ahead == last)
+        def _():
+            for r in range(UNIT):
+                for k in range(1, chips):
+                    far_last(r, k, b).start()
 
         near_copy(j, 0, sibling).wait_recv()
         for k in range(1, chips):

time: 186 us -> 218 us (1.17)
  Pallas kernels: 183 us -> 215 us
    pallas_call x1, Pallas kernels: 183 us -> 215 us  [on_device(): pl.pallas_call(functools.partial(kernel, n, s), out_shape=pltpu.VMEM((nb,...]
where the time goes in v6:
time: 218 us
  Pallas kernels  215 us (99%)
  local copies, waits for them, and re-layouts  3.22 us (1%)
    pallas_call x1, Pallas kernels, on_device(): pl.pallas_call(functools.partial(kernel, n, s), out_shape=pltpu.VMEM((nb,...  215 us

profile of v6, /device:TPU:1, one launch (start us, length us, event | category | flops | bytes accessed | tf_op | source)
XLA Modules:
  0.0 218.0 jit_solution(11059251955535313733)
XLA Ops:
  0.0 214.8 %wave_step.1 = f32[192,40,256]{2,1,0:T(8,128)S(1)} custom-call(f32[192,40,256]{2,1,0:T(8,128)} %spec.1, s32[40,256]{1,0:T(8,128)} %mask_h.1, f32[40,256]{1,0:T(8,128)} %speed_h.1, f32[40,256]{1,0:T(8,128)} %heading_h.1, bf16[768,768]{1,0:T(8,128)(2,1)} %quad.1, f32[768,128]{1,0:T(8,128)} %constant.2.clone.table), custom_call_target="tpu_custom_call" | custom-call | flops 6039797760 | bytes 15728640 | tf_op jit(solution)/shard_map/wave_step/pallas_call | solution.py:459
  214.8 3.2 %copy.8 = f32[192,40,256]{2,1,0:T(8,128)} copy(f32[192,40,256]{2,1,0:T(8,128)S(1)} %wave_step.1) | data formatting | bytes 15728640
